TPU v7x, 32 devices: a whole 2x2x4 slice. The times are simulated.
32 devices in a mesh: groups: 2 (over x), dp: 4 (over y, core), expert: 4 (over z).
Axes of the slice: x: 2, y: 2, z: 4, core: 2. Of those that a mesh axis runs over, the one named last changes fastest.
Arguments:
- query: bfloat16 [128, 4096], P(('groups', 'dp', 'expert')), parts along dimension 0, may hold values from -27 to 27
- fresh_kv: bfloat16 [128, 512], P(('groups', 'dp', 'expert')), parts along dimension 0, may hold values from -16 to 16
- cache: bfloat16 [128, 512, 512], P(('groups', 'dp', 'expert')), parts along dimension 0, may hold values from -6 to 6
- lengths: int32 [128], P(('groups', 'dp', 'expert')), parts along dimension 0, may hold values from 2 to 512, as said below
- moves: int32 [8, 4], P('groups'), parts along dimension 0, may hold values from 0 to 3, as said below
- residual: bfloat16 [128, 4096], P(('groups', 'dp', 'expert')), parts along dimension 0, may hold values from -4 to 4
- out_weight: bfloat16 [4096, 4096], P('expert'), may hold values from -0.09375 to 0.09375
- norm_gain: float32 [4096], replicated, may hold values from 0.1 to 1.9
- w_gate: bfloat16 [4, 4096, 1536], P('dp', None, 'expert'), may hold values from -0.09375 to 0.09375
- w_up: bfloat16 [4, 4096, 1536], P('dp', None, 'expert'), may hold values from -0.09375 to 0.09375
- w_down: bfloat16 [4, 1536, 4096], P('dp', 'expert'), may hold values from -0.15625 to 0.15625
- routes: int32 [128, 2], P(('groups', 'dp', 'expert')), parts along dimension 0, may hold values from 0 to 3, all different within a row; in each aligned block of 4 rows (0 to 3, 4 to 7, ...) at most 3 rows name the same one
- gates: float32 [128, 2], P(('groups', 'dp', 'expert')), parts along dimension 0, may hold values from 0.05 to 0.5
Outputs:
- layer_out: bfloat16 [128, 4096], P(('groups', 'dp', 'expert')), parts along dimension 0
There are 2 independent parts, one for each index of `groups`. A program takes and returns all parts, laid end to end along the dimension named above; an argument that names none is the same for every part. Nothing has to cross between parts.
Inputs may be any that keep to these rules, and one draw needn't show every extreme that they name: `lengths`: slot 0 of every device (the first of its 4 rows) holds 512 cached positions; other requests 2 to 512. For each expert index e, d -> moves[e, d] is one cycle through all 4 dp indices. `routes`: each row names 2 different experts; in the 4 rows of one device no expert is named by more than 3 rows, and in some device one expert is named by exactly 3.
All inputs are finite; a program needn't handle non-finite values.
Results may differ from a plain program's by a relative error of at most 0.0055.
Values may be sent and summed in bfloat16 or wider, within the bound.
A program may use at most 128 MiB of HBM per device.

v0:
```python
import jax
import jax.numpy as jnp
from jax import lax
from jax.sharding import PartitionSpec as P

D = 4096
HD = 128
QH = 32
KVH = 2
CTX = 512
CAP = 3


norm_eps = 1e-06


def cache_part(queries, entries, lengths_used):
    count_rows = queries.shape[0]
    group_size = QH // KVH
    query_heads = queries.reshape(count_rows, KVH, group_size, HD)
    keys_all = entries[:, :, : KVH * HD].reshape(count_rows, CTX, KVH, HD)
    values_all = entries[:, :, KVH * HD :].reshape(count_rows, CTX, KVH, HD)
    scores = jnp.einsum(
        "nhgd,nchd->nhgc", query_heads, keys_all, preferred_element_type=jnp.float32
    ) * HD ** (-0.5)
    valid_mask = (jnp.arange(CTX, dtype=jnp.int32)[None, :] < lengths_used[:, None])[
        :, None, None, :
    ]
    scores = jnp.where(valid_mask, scores, -1e30)
    row_max = jnp.max(scores, axis=-1)
    weights_raw = jnp.where(valid_mask, jnp.exp(scores - row_max[..., None]), 0.0)
    row_sum = jnp.sum(weights_raw, axis=-1)
    rounded = weights_raw.astype(jnp.bfloat16)
    out_cache = jnp.einsum(
        "nhgc,nchd->nhgd", rounded, values_all, preferred_element_type=jnp.float32
    )
    return (
        out_cache.reshape(count_rows, QH * HD),
        row_max.reshape(count_rows, QH),
        row_sum.reshape(count_rows, QH),
    )


def combine_own(out_cache, row_max, row_sum, queries, fresh):
    count_rows = queries.shape[0]
    group_size = QH // KVH
    query_heads = queries.astype(jnp.float32).reshape(count_rows, KVH, group_size, HD)
    own_keys = fresh[:, : KVH * HD].astype(jnp.float32).reshape(count_rows, KVH, 1, HD)
    own_values = fresh[:, KVH * HD :].astype(jnp.float32).reshape(count_rows, KVH, 1, HD)
    own_score = jnp.sum(query_heads * own_keys, axis=-1) * HD ** (-0.5)
    max_heads = row_max.reshape(count_rows, KVH, group_size)
    sum_heads = row_sum.reshape(count_rows, KVH, group_size)
    top_score = jnp.maximum(max_heads, own_score)
    cache_factor = jnp.exp(max_heads - top_score)
    own_factor = jnp.exp(own_score - top_score)
    numer = (
        cache_factor[..., None] * out_cache.reshape(count_rows, KVH, group_size, HD)
        + own_factor[..., None] * own_values
    )
    denom = cache_factor * sum_heads + own_factor
    return (numer / denom[..., None]).reshape(count_rows, QH * HD).astype(jnp.bfloat16)


def per_device(
    query,
    fresh_kv,
    cache,
    lengths,
    moves,
    residual,
    out_weight,
    norm_gain,
    w_gate,
    w_up,
    w_down,
    routes,
    gates,
):
    dp_count = lax.axis_size("dp")
    ex_count = lax.axis_size("expert")
    dp_index = lax.axis_index("dp")
    ex_index = lax.axis_index("expert")
    move_row = lax.dynamic_index_in_dim(moves, ex_index, 0, keepdims=False)
    target = lax.dynamic_index_in_dim(move_row, dp_index, 0, keepdims=False)
    peer_ids = jnp.arange(dp_count, dtype=jnp.int32)
    source = jnp.sum(jnp.where(move_row == dp_index, peer_ids, 0))
    outgoing = jnp.where(
        (peer_ids == target)[:, None, None], cache[0][None], jnp.zeros((), cache.dtype)
    )
    arrived = lax.all_to_all(outgoing, "dp", split_axis=0, concat_axis=0, tiled=True)
    incoming = lax.dynamic_index_in_dim(arrived, source, 0, keepdims=True)
    resident = jnp.concatenate([incoming, cache[1:]], axis=0)
    out_cache, row_max, row_sum = cache_part(query, resident, lengths)
    attended = combine_own(out_cache, row_max, row_sum, query, fresh_kv)
    blocks = lax.all_to_all(attended, "expert", split_axis=1, concat_axis=0, tiled=True)
    projected = lax.psum_scatter(
        jnp.dot(blocks, out_weight, preferred_element_type=jnp.float32),
        "expert",
        scatter_dimension=0,
        tiled=True,
    )
    hidden = residual.astype(jnp.float32) + projected
    normed = (
        hidden * lax.rsqrt(jnp.mean(hidden * hidden, axis=-1, keepdims=True) + norm_eps) * norm_gain
    ).astype(jnp.bfloat16)
    token_count = routes.shape[0]
    top_count = routes.shape[1]
    flat_routes = routes.reshape(-1)
    hit_table = (flat_routes[:, None] == jnp.arange(dp_count, dtype=jnp.int32)[None, :]).astype(
        jnp.int32
    )
    before = jnp.cumsum(hit_table, axis=0) - hit_table
    position = jnp.sum(before * hit_table, axis=-1)
    slot_ids = flat_routes * CAP + position
    slot_match = (
        jnp.arange(dp_count * CAP, dtype=jnp.int32)[:, None] == slot_ids[None, :]
    ).reshape(dp_count * CAP, token_count, top_count)
    dispatch = jnp.sum(slot_match.astype(jnp.int32), axis=-1).astype(jnp.bfloat16)
    combine_table = jnp.sum(jnp.where(slot_match, gates[None, :, :], 0.0), axis=-1).T
    sendrows = jnp.dot(dispatch, normed, preferred_element_type=jnp.float32).astype(jnp.bfloat16)
    spread = jnp.broadcast_to(
        sendrows.reshape(dp_count, 1, CAP, D), (dp_count, ex_count, CAP, D)
    ).reshape(dp_count * ex_count, CAP, D)
    arrived_rows = lax.all_to_all(spread, ("dp", "expert"), split_axis=0, concat_axis=0, tiled=True)
    row_block = arrived_rows.reshape(-1, D)
    gate_val = jnp.dot(row_block, w_gate[0], preferred_element_type=jnp.float32)
    up_val = jnp.dot(row_block, w_up[0], preferred_element_type=jnp.float32)
    activation = (jax.nn.silu(gate_val) * up_val).astype(jnp.bfloat16)
    partial_value = jnp.dot(activation, w_down[0], preferred_element_type=jnp.float32).reshape(
        dp_count * ex_count, CAP, D
    )
    returned_rows = lax.all_to_all(
        partial_value.astype(jnp.bfloat16),
        ("dp", "expert"),
        split_axis=0,
        concat_axis=0,
        tiled=True,
    ).astype(partial_value.dtype)
    summed = jnp.sum(returned_rows.reshape(dp_count, ex_count, CAP, D), axis=1)
    mixture = jnp.dot(
        combine_table,
        summed.reshape(dp_count * CAP, D),
        precision=lax.Precision.HIGHEST,
        preferred_element_type=jnp.float32,
    )
    return (hidden + mixture).astype(jnp.bfloat16)


def solution(mesh):
    placed = (
        P(("groups", "dp", "expert"), None),
        P(("groups", "dp", "expert"), None),
        P(("groups", "dp", "expert"), None, None),
        P(("groups", "dp", "expert")),
        P("groups", None),
        P(("groups", "dp", "expert"), None),
        P("expert", None),
        P(),
        P("dp", None, "expert"),
        P("dp", None, "expert"),
        P("dp", "expert", None),
        P(("groups", "dp", "expert"), None),
        P(("groups", "dp", "expert"), None),
    )
    return jax.shard_map(
        per_device,
        mesh=mesh,
        in_specs=placed,
        out_specs=P(("groups", "dp", "expert"), None),
        check_vma=False,
    )
```

profile of v0, /device:TPU:0, one launch (start us, length us, event | category | flops | bytes accessed | tf_op | source)
XLA Modules:
  0.0 161.4 jit_solution(8375357296587837905)
XLA Ops:
  6.5 1.4 dynamic_slice.12
  8.6 1.9 %slice_bitcast_fusion = bf16[512,512]{1,0:T(8,128)(2,1)} fusion(bf16[4,512,512]{2,1,0:T(8,128)(2,1)} %param.15), kind=kLoop, calls=%fused_computation.24 | loop fusion | bytes 1048576 | tf_op jit(solution)/shard_map/jit(_where)/broadcast_in_dim | solution.py:87
  10.5 2.1 %copy.39 = bf16[512,512]{0,1:T(8,128)(2,1)} copy(bf16[512,512]{1,0:T(8,128)(2,1)} %slice_bitcast_fusion) | data formatting | bytes 1048576 | tf_op jit(solution)/shard_map/jit(_where)/broadcast_in_dim | solution.py:87
  12.5 2.6 %broadcast_select_fusion = bf16[4,512,512]{1,2,0:T(8,128)(2,1)} fusion(pred[4]{0:T(512)(128)(4,1)S(1)} %iota_compare_fusion.3, bf16[512,512]{0,1:T(8,128)(2,1)} %copy.39), kind=kLoop, calls=%fused_computation.11 | loop fusion | flops 1048576 | bytes 2621444 | tf_op jit(solution)/shard_map/jit(_where)/select_n | solution.py:87
  15.2 4.4 %all-to-all-start = ((bf16[4,512,512]{1,2,0:T(8,128)(2,1)}), bf16[4,512,512]{1,2,0:T(8,128)(2,1)}, u32[]{:S(2)}, u32[]{:S(2)}) async-start(bf16[4,512,512]{1,2,0:T(8,128)(2,1)} %broadcast_select_fusion), calls=%async_computation | async-start | bytes 4194304 | tf_op jit(solution)/shard_map/all_to_all | solution.py:90
  19.6 1.3 fusion.31
  22.2 2.7 %slice.19 = bf16[3,512,512]{2,1,0:T(8,128)(2,1)} slice(bf16[4,512,512]{2,1,0:T(8,128)(2,1)} %param.15), slice={[1:4], [0:512], [0:512]} | slice | bytes 3145728 | tf_op jit(solution)/shard_map/slice | solution.py:92
  25.0 2.7 %copy.54 = bf16[3,512,512]{1,2,0:T(8,128)(2,1)} copy(bf16[3,512,512]{2,1,0:T(8,128)(2,1)} %slice.19) | data formatting | bytes 3145728
  28.9 17.1 %all-to-all-done = bf16[4,512,512]{1,2,0:T(8,128)(2,1)} async-done(((bf16[4,512,512]{1,2,0:T(8,128)(2,1)}), bf16[4,512,512]{1,2,0:T(8,128)(2,1)}, u32[]{:S(2)}, u32[]{:S(2)}) %all-to-all-start) | async-done | bytes 2097184 | tf_op jit(solution)/shard_map/all_to_all | solution.py:90
  47.1 1.6 fusion.17
  50.4 5.7 %all-to-all-start.1 = ((bf16[4,4,1024]{2,0,1:T(4,128)(2,1)}), bf16[4,4,1024]{2,0,1:T(4,128)(2,1)S(1)}, u32[]{:S(2)}, u32[]{:S(2)}) async-start(bf16[4,4,1024]{2,0,1:T(4,128)(2,1)} %copy.43), calls=%async_computation.1 | async-start | bytes 65536 | tf_op jit(solution)/shard_map/all_to_all | solution.py:95
  56.2 5.5 %all-to-all-done.1 = bf16[4,4,1024]{2,0,1:T(4,128)(2,1)S(1)} async-done(((bf16[4,4,1024]{2,0,1:T(4,128)(2,1)}), bf16[4,4,1024]{2,0,1:T(4,128)(2,1)S(1)}, u32[]{:S(2)}, u32[]{:S(2)}) %all-to-all-start.1) | async-done | bytes 32800 | tf_op jit(solution)/shard_map/all_to_all | solution.py:95
  61.8 5.3 %fusion.37 = f32[16,4096]{1,0:T(8,128)} fusion(bf16[16,1024]{1,0:T(8,128)(2,1)S(1)} %all_to_all.24, bf16[1024,4096]{1,0:T(8,128)(2,1)} %param.19), kind=kOutput, calls=%fused_computation.62 | convolution fusion | flops 134217728 | bytes 8683520 | tf_op jit(solution)/shard_map/dot_general | solution.py:97
  68.5 31.5 %all-reduce.3.cloned.1.call-done = f32[16,4096]{1,0:T(8,128)} async-done(((f32[16,4096]{1,0:T(8,128)}), f32[16,4096]{1,0:T(8,128)}) %all-reduce.3.cloned.1.call-update) | async-done | bytes 262160
  101.1 1.1 convolution_convert_fusion.1
  102.5 20.0 %all_to_all.31 = bf16[16,3,4096]{2,1,0:T(4,128)(2,1)} all-to-all(bf16[16,3,4096]{2,1,0:T(4,128)(2,1)S(1)} %bitcast.46), channel_id=1, replica_groups=mesh['groups'=2,'dp'=4,'expert'=4] {'dp','expert'}, dimensions={0} | all-to-all | bytes 786432 | tf_op jit(solution)/shard_map/all_to_all | solution.py:124
  122.5 1.4 reshape.124
  123.9 2.6 %fusion.4 = f32[48,384]{1,0:T(8,128)S(1)} fusion(bf16[48,4096]{1,0:T(8,128)(2,1)S(1)} %reshape.124, bf16[1,4096,384]{2,1,0:T(8,128)(2,1)} %param.21), kind=kOutput, calls=%fused_computation.7 | convolution fusion | flops 150994944 | bytes 3612672 | tf_op jit(solution)/shard_map/dot_general | solution.py:126
  126.8 1.2 fusion.13
  129.4 1.2 copy.48
  130.6 4.2 %all-to-all-start.3 = ((bf16[16,3,4096]{2,1,0:T(4,128)(2,1)}), bf16[16,3,4096]{2,1,0:T(4,128)(2,1)}, u32[]{:S(2)}, u32[]{:S(2)}) async-start(bf16[16,3,4096]{2,1,0:T(4,128)(2,1)} %copy.48), calls=%async_computation.3 | async-start | bytes 1048576 | tf_op jit(solution)/shard_map/all_to_all | solution.py:132
  134.9 15.6 %all-to-all-done.3 = bf16[16,3,4096]{2,1,0:T(4,128)(2,1)} async-done(((bf16[16,3,4096]{2,1,0:T(4,128)(2,1)}), bf16[16,3,4096]{2,1,0:T(4,128)(2,1)}, u32[]{:S(2)}, u32[]{:S(2)}) %all-to-all-start.3) | async-done | bytes 393248 | tf_op jit(solution)/shard_map/all_to_all | solution.py:132
  150.5 1.4 convert_reduce_fusion
  152.7 1.9 %fusion = bf16[4,4096]{1,0:T(4,128)(2,1)} fusion(f32[12,4]{0,1:T(4,128)S(1)} %select_reduce_fusion, f32[12,4096]{1,0:T(8,128)} %reshape.127, f32[16,4096]{1,0:T(8,128)} %all-reduce.3.cloned.1.call-done, u32[]{:T(128)S(6)} %multiply.7, bf16[4,4096]{1,0:T(4,128)(2,1)S(1)} %copy-done.3), kind=kOutput, calls=%fused_computation.3 | convolution fusion | flops 2424832 | bytes 327876 | tf_op jit(solution)/shard_map/dot_general | solution.py:140
  (57 shorter events, 8.8 us)
Async XLA Ops:
  6.5 122.2 %copy-start = (bf16[1,384,4096]{2,1,0:T(8,128)(2,1)S(1)}, bf16[1,384,4096]{2,1,0:T(8,128)(2,1)}, u32[]{:S(2)}) copy-start(bf16[1,384,4096]{2,1,0:T(8,128)(2,1)} %param.23) | copy-start | bytes 9437188
  15.2 30.9 %all-to-all-start = ((bf16[4,512,512]{1,2,0:T(8,128)(2,1)}), bf16[4,512,512]{1,2,0:T(8,128)(2,1)}, u32[]{:S(2)}, u32[]{:S(2)}) async-start(bf16[4,512,512]{1,2,0:T(8,128)(2,1)} %broadcast_select_fusion), calls=%async_computation | async-start | bytes 4194304 | tf_op jit(solution)/shard_map/all_to_all | solution.py:90
  24.9 2.7 %copy-start.4 = (bf16[4,4096]{1,0:T(4,128)(2,1)S(1)}, bf16[4,4096]{1,0:T(4,128)(2,1)}, u32[]{:S(2)}) copy-start(bf16[4,4096]{1,0:T(4,128)(2,1)} %param.13) | copy-start | bytes 98308
  24.9 2.7 %copy-start.6 = (bf16[4,512]{1,0:T(4,128)(2,1)S(1)}, bf16[4,512]{1,0:T(4,128)(2,1)}, u32[]{:S(2)}) copy-start(bf16[4,512]{1,0:T(4,128)(2,1)} %param.14) | copy-start | bytes 12292
  25.0 2.7 %copy-start.7 = (s32[4,2]{0,1:T(2,128)S(1)}, s32[4,2]{0,1:T(2,128)}, u32[]{:S(2)}) copy-start(s32[4,2]{0,1:T(2,128)} %param.24) | copy-start | bytes 100
  25.0 3.9 %copy-start.9 = (s32[4]{0:T(128)S(1)}, s32[4]{0:T(128)}, u32[]{:S(2)}) copy-start(s32[4]{0:T(128)} %param.16) | copy-start | bytes 52
  50.4 11.3 %all-to-all-start.1 = ((bf16[4,4,1024]{2,0,1:T(4,128)(2,1)}), bf16[4,4,1024]{2,0,1:T(4,128)(2,1)S(1)}, u32[]{:S(2)}, u32[]{:S(2)}) async-start(bf16[4,4,1024]{2,0,1:T(4,128)(2,1)} %copy.43), calls=%async_computation.1 | async-start | bytes 65536 | tf_op jit(solution)/shard_map/all_to_all | solution.py:95
  56.0 43.9 %all-reduce.3.cloned.1.call-start = ((), (), s32[]{:S(2)}) async-start(), calls=%async_computation.4 | async-start | bytes 524288
  61.7 5.5 %copy-start.10 = (u32[32]{0:T(128)S(1)}, u32[32]{0:T(128)}, u32[]{:S(2)}) copy-start(u32[32]{0:T(128)} %constant.70) | copy-start | bytes 388
  61.7 38.3 %copy-start.2 = (bf16[4,4096]{1,0:T(4,128)(2,1)S(1)}, bf16[4,4096]{1,0:T(4,128)(2,1)}, u32[]{:S(2)}) copy-start(bf16[4,4096]{1,0:T(4,128)(2,1)} %param.18) | copy-start | bytes 98308
  61.7 39.3 %copy-start.5 = (f32[4096]{0:T(1024)S(1)}, f32[4096]{0:T(1024)}, u32[]{:S(2)}) copy-start(f32[4096]{0:T(1024)} %param.20) | copy-start | bytes 49156
  123.9 2.8 %copy-start.1 = (bf16[1,4096,384]{2,1,0:T(8,128)(2,1)S(1)}, bf16[1,4096,384]{2,1,0:T(8,128)(2,1)}, u32[]{:S(2)}) copy-start(bf16[1,4096,384]{2,1,0:T(8,128)(2,1)} %param.22) | copy-start | bytes 9437188
  128.7 6.1 %copy-start.8 = (f32[4,2]{0,1:T(2,128)S(1)}, f32[4,2]{0,1:T(2,128)}, u32[]{:S(2)}) copy-start(f32[4,2]{0,1:T(2,128)} %param.25) | copy-start | bytes 100
  129.4 23.2 %copy-start.3 = (bf16[4,4096]{1,0:T(4,128)(2,1)S(1)}, bf16[4,4096]{1,0:T(4,128)(2,1)}, u32[]{:S(2)}) copy-start(bf16[4,4096]{1,0:T(4,128)(2,1)} %param.18) | copy-start | bytes 98308
  130.6 19.9 %all-to-all-start.3 = ((bf16[16,3,4096]{2,1,0:T(4,128)(2,1)}), bf16[16,3,4096]{2,1,0:T(4,128)(2,1)}, u32[]{:S(2)}, u32[]{:S(2)}) async-start(bf16[16,3,4096]{2,1,0:T(4,128)(2,1)} %copy.48), calls=%async_computation.3 | async-start | bytes 1048576 | tf_op jit(solution)/shard_map/all_to_all | solution.py:132
Sparse Core Ops, SparseCore 0:
  67.2 32.7 all-reduce.2
where the time goes:
time: 162 us; the launch traced here: 161 us
  waiting for transfers between devices  69.8 us (43%)
  blocking collectives  20 us (12%)
  local copies, waits for them, and re-layouts  18.1 us (11%)
  between operations  16.2 us (10%)
  starting transfers between devices  14.4 us (9%)
  matrix products  13.5 us (8%)
  other arithmetic  9.41 us (6%)
    unnamed x2, waiting for transfers between devices  31.5 us
    all_to_all x1, blocking collectives, per_device(): lax.all_to_all(spread, ('dp', 'expert'), split_axis=0, concat_axis=0, til...  20 us
    all_to_all x1, waiting for transfers between devices, per_device(): lax.all_to_all(outgoing, 'dp', split_axis=0, concat_axis=0, tiled=True)  17.1 us
    all_to_all x1, waiting for transfers between devices, per_device(): lax.all_to_all(partial_value.astype(jnp.bfloat16), ('dp', 'expert'), spli...  15.6 us
    all_to_all x1, starting transfers between devices, per_device(): lax.all_to_all(attended, 'expert', split_axis=1, concat_axis=0, tiled=True)  5.67 us
    all_to_all x1, waiting for transfers between devices, per_device(): lax.all_to_all(attended, 'expert', split_axis=1, concat_axis=0, tiled=True)  5.55 us
    dot_general x1, matrix products, per_device(): jnp.dot(blocks, out_weight, preferred_element_type=jnp.float32)  5.29 us
    all_to_all x1, starting transfers between devices, per_device(): lax.all_to_all(outgoing, 'dp', split_axis=0, concat_axis=0, tiled=True)  4.45 us
  transfers between devices with their start and end apart: 4, of which 4 were waited for; matrix products, arithmetic and copies ran while one was open for 5% of the time, Pallas kernels for 0%

commit v1 on v0

v1 whole, which is shorter than its diff:
```python
import functools

import jax
import jax.numpy as jnp
from jax import lax
from jax.experimental import pallas as pl
from jax.experimental.pallas import tpu as pltpu
from jax.sharding import PartitionSpec as P

HD = 128
KVH = 2
NORM_EPS = 1e-06
F32 = jnp.float32
BF16 = jnp.bfloat16


def layer_kernel(
    dp,
    ex,
    lengths,
    moves,
    query,
    fresh,
    residual,
    routes,
    gates,
    gain,
    cache_hbm,
    wo_hbm,
    wg_hbm,
    wu_hbm,
    wd_hbm,
    out,
    cache,
    wo,
    wg,
    wu,
    wd,
    qf,
    q_send,
    q_recv,
    r_send,
    r_recv,
    a_send,
    a0_send,
    a0_recv,
    a_recv,
    a_all,
    p_send,
    p_recv,
    hid,
    x_send,
    s_send,
    x_all,
    s_all,
    y_send,
    y_recv,
    total,
    fold,
    z_send,
    z_recv,
    local_sem,
    q_s,
    q_r,
    r_s,
    r_r,
    a_s,
    a_r,
    a0_s,
    a0_r,
    p_s,
    p_r,
    x_s,
    x_r,
    s_s,
    s_r,
    x2_s,
    x2_r,
    s2_s,
    s2_r,
    y_s,
    y_r,
    z_s,
    z_r,
):
    d = lax.axis_index("dp")
    e = lax.axis_index("expert")
    n = dp * ex
    me = d * ex + e
    rows = query.shape[0]
    width = query.shape[1]
    heads = width // HD
    group = heads // KVH
    hk = heads // ex
    ctx = cache.shape[1]
    part = width // ex
    tiles = part // HD
    tokens = rows * ex
    top = routes.shape[1]
    pieces = 16 // rows
    piece = width // pieces

    def copy(src, dst, ss, rs, dd, ee):
        return pltpu.make_async_remote_copy(
            src_ref=src,
            dst_ref=dst,
            send_sem=ss,
            recv_sem=rs,
            device_id={"dp": dd, "expert": ee},
            device_id_type=pl.DeviceIdType.MESH,
        )

    barrier = pltpu.get_barrier_semaphore()

    def greet(o, c):
        p = lax.rem(me + o, n)
        pl.semaphore_signal(
            barrier,
            inc=1,
            device_id={"dp": p // ex, "expert": lax.rem(p, ex)},
            device_id_type=pl.DeviceIdType.MESH,
        )
        return c

    lax.fori_loop(1, n, greet, 0)

    local = [
        pltpu.make_async_copy(cache_hbm, cache, local_sem.at[0]),
        pltpu.make_async_copy(wo_hbm, wo, local_sem.at[1]),
        pltpu.make_async_copy(wg_hbm.at[0], wg, local_sem.at[2]),
        pltpu.make_async_copy(wu_hbm.at[0], wu, local_sem.at[3]),
        pltpu.make_async_copy(wd_hbm.at[0], wd, local_sem.at[4]),
    ]
    for c in local:
        c.start()

    for h in range(heads):
        qf[:, h, :] = query[:, h * HD : (h + 1) * HD].astype(F32)
    for i in range(2 * KVH):
        qf[:, heads + i, :] = fresh[:, i * HD : (i + 1) * HD].astype(F32)
    pad = qf.shape[1] - heads - 2 * KVH
    qf[:, heads + 2 * KVH :, :] = jnp.zeros((rows, pad, HD), F32)
    q_send[...] = qf[0].astype(BF16)

    lane = lax.broadcasted_iota(jnp.int32, (rows, HD), 1)
    table = jnp.zeros((rows, HD), F32)
    for k in range(top):
        table += jnp.where(lane == routes[:, k : k + 1], gates[:, k : k + 1], 0.0)
    for k in range(ex):
        for j in range(tiles):
            r_send[k, :, j, :] = residual[
                :, k * part + j * HD : k * part + (j + 1) * HD
            ].astype(F32)
        r_send[k, :, tiles, :] = table

    pl.semaphore_wait(barrier, n - 1)

    sends = []

    def exchange(count, me_, make):
        made = [make(lax.rem(me_ + o, count)) for o in range(1, count)]
        for c in made:
            c.start()
        sends.extend(made)

    exchange(dp, d, lambda p: copy(q_send, q_recv.at[d], q_s.at[p], q_r.at[d], p, e))
    exchange(
        ex,
        e,
        lambda p: copy(
            r_send.at[p], r_recv.at[pl.ds(e * rows, rows)], r_s.at[p], r_r.at[e], d, p
        ),
    )
    q_recv[d] = q_send[...]
    r_recv[pl.ds(e * rows, rows)] = r_send[e]

    head = lax.broadcasted_iota(jnp.int32, (heads, 1), 0)
    first = head < group

    def attend(r, q_all):
        q = q_all[:heads]
        own_key = jnp.where(first, q_all[heads : heads + 1], q_all[heads + 1 : heads + 2])
        own_value = jnp.where(
            first, q_all[heads + 2 : heads + 3], q_all[heads + 3 : heads + 4]
        )
        wide = jnp.concatenate(
            [jnp.where(first, q, 0.0), jnp.where(first, 0.0, q)], axis=1
        ).astype(BF16)
        scores = lax.dot_general(
            wide,
            cache[r, :, : KVH * HD],
            (((1,), (1,)), ((), ())),
            preferred_element_type=F32,
        ) * HD ** (-0.5)
        position = lax.broadcasted_iota(jnp.int32, (heads, ctx), 1)
        valid = position < lengths[r]
        scores = jnp.where(valid, scores, -1e30)
        cache_max = jnp.max(scores, axis=-1, keepdims=True)
        weights = jnp.where(valid, jnp.exp(scores - cache_max), 0.0)
        cache_sum = jnp.sum(weights, axis=-1, keepdims=True)
        both = jnp.dot(
            weights.astype(BF16), cache[r, :, KVH * HD :], preferred_element_type=F32
        )
        cache_out = jnp.where(first, both[:, :HD], both[:, HD:])
        own_score = jnp.sum(q * own_key, axis=-1, keepdims=True) * HD ** (-0.5)
        top_score = jnp.maximum(cache_max, own_score)
        f_cache = jnp.exp(cache_max - top_score)
        f_own = jnp.exp(own_score - top_score)
        return (f_cache * cache_out + f_own * own_value) / (f_cache * cache_sum + f_own)

    local[0].wait()

    def stay(r, c):
        att = attend(r, qf[r])
        for k in range(ex):
            a_send[k, r - 1] = att[k * hk : (k + 1) * hk]
        return c

    lax.fori_loop(1, rows, stay, 0)
    exchange(
        ex,
        e,
        lambda p: copy(
            a_send.at[p],
            a_recv.at[pl.ds(e * rows + 1, rows - 1)],
            a_s.at[p],
            a_r.at[e],
            d,
            p,
        ),
    )
    a_recv[pl.ds(e * rows + 1, rows - 1)] = a_send[e]

    for o in range(1, dp):
        p = lax.rem(d + o, dp)
        copy(q_send, q_recv.at[p], q_s.at[p], q_r.at[p], p, e).wait_recv()
    target = moves[e, d]
    q0 = jnp.zeros(q_send.shape, F32)
    for j in range(dp):
        q0 += jnp.where(target == j, q_recv[j].astype(F32), 0.0)
    att = attend(0, q0)
    for k in range(ex):
        a0_send[k] = att[k * hk : (k + 1) * hk]

    def a0_copy(o, source):
        p = lax.rem(me + o, n)
        pd, pk = p // ex, lax.rem(p, ex)
        sd, sk = (d, e) if not source else (pd, pk)
        slot = me if not source else p
        return copy(
            a0_send.at[pk], a0_recv.at[sd, sk], a0_s.at[p], a0_r.at[slot], pd, pk
        )

    def a0_start(o, c):
        a0_copy(o, False).start()
        return c

    lax.fori_loop(1, n, a0_start, 0)
    a0_recv[d, e] = a0_send[e]

    for o in range(1, ex):
        p = lax.rem(e + o, ex)
        copy(
            r_send.at[p], r_recv.at[pl.ds(p * rows, rows)], r_s.at[p], r_r.at[p], d, p
        ).wait_recv()
        copy(
            a_send.at[p],
            a_recv.at[pl.ds(p * rows + 1, rows - 1)],
            a_s.at[p],
            a_r.at[p],
            d,
            p,
        ).wait_recv()

    def a0_wait(o, c):
        a0_copy(o, True).wait_recv()
        return c

    local[1].wait()
    lax.fori_loop(1, n, a0_wait, 0)
    for k in range(ex):
        chosen = jnp.zeros((hk, HD), F32)
        for j in range(dp):
            chosen += jnp.where(moves[k, j] == d, a0_recv[j, k], 0.0)
        a_recv[k * rows] = chosen
    for h in range(hk):
        a_all[:, h * HD : (h + 1) * HD] = a_recv[:, h, :].astype(BF16)

    def project(k):
        return jnp.dot(
            a_all[...],
            wo[:, pl.ds(pl.multiple_of(k * part, HD), part)],
            preferred_element_type=F32,
        )

    for o in range(1, ex):
        p = lax.rem(e + o, ex)
        p_send[p] = project(p).astype(BF16)
        c = copy(p_send.at[p], p_recv.at[e], p_s.at[p], p_r.at[e], d, p)
        c.start()
        sends.append(c)
    hid[...] = project(e)
    for j in range(tiles):
        hid[:, j * HD : (j + 1) * HD] += r_recv[:, j, :]
    for o in range(1, ex):
        p = lax.rem(e + o, ex)
        copy(p_send.at[p], p_recv.at[p], p_s.at[p], p_r.at[p], d, p).wait_recv()
        hid[...] += p_recv[p].astype(F32)

    hidden = hid[...]
    squares = jnp.sum(hidden * hidden, axis=-1, keepdims=True)
    last = lax.broadcasted_iota(jnp.int32, (tokens, HD), 1) == HD - 1
    s_send[...] = jnp.where(last, squares, r_recv[:, tiles, :])
    x_send[...] = (
        hidden * gain[:, pl.ds(pl.multiple_of(e * part, HD), part)]
    ).astype(BF16)

    def x_at(dd, ee):
        return x_all.at[
            pl.ds(pl.multiple_of(dd * tokens, 16), tokens),
            pl.ds(pl.multiple_of(ee * part, HD), part),
        ]

    exchange(ex, e, lambda p: copy(x_send, x_at(d, e), x_s.at[p], x_r.at[e], d, p))
    exchange(
        ex, e, lambda p: copy(s_send, s_all.at[d, e], s_s.at[p], s_r.at[e], d, p)
    )
    x_at(d, e)[...] = x_send[...]
    s_all[d, e] = s_send[...]
    for o in range(1, ex):
        p = lax.rem(e + o, ex)
        copy(x_send, x_at(d, p), x_s.at[p], x_r.at[p], d, p).wait_recv()
        copy(s_send, s_all.at[d, p], s_s.at[p], s_r.at[p], d, p).wait_recv()

    def x_rows(dd):
        return x_all.at[pl.ds(pl.multiple_of(dd * tokens, 16), tokens)]

    exchange(dp, d, lambda p: copy(x_rows(d), x_rows(d), x2_s.at[p], x2_r.at[d], p, e))
    exchange(
        dp, d, lambda p: copy(s_all.at[d], s_all.at[d], s2_s.at[p], s2_r.at[d], p, e)
    )
    local[2].wait()
    local[3].wait()
    for o in range(1, dp):
        p = lax.rem(d + o, dp)
        copy(x_rows(p), x_rows(p), x2_s.at[p], x2_r.at[p], p, e).wait_recv()
        copy(s_all.at[p], s_all.at[p], s2_s.at[p], s2_r.at[p], p, e).wait_recv()

    every = dp * tokens
    wide_lane = lax.broadcasted_iota(jnp.int32, (every, HD), 1)
    stats = s_all[:, 0].reshape(every, HD)
    weight = jnp.sum(jnp.where(wide_lane == d, stats, 0.0), axis=-1, keepdims=True)
    for k in range(1, ex):
        stats += s_all[:, k].reshape(every, HD)
    mean = (
        jnp.sum(jnp.where(wide_lane == HD - 1, stats, 0.0), axis=-1, keepdims=True)
        / width
    )
    scale = lax.rsqrt(mean + NORM_EPS)
    gate_val = jnp.dot(x_all[...], wg[...], preferred_element_type=F32) * scale
    up_val = jnp.dot(x_all[...], wu[...], preferred_element_type=F32) * scale
    act = (gate_val / (1.0 + jnp.exp(-gate_val)) * up_val).astype(BF16)

    local[4].wait()

    def y_copy(p, src, c):
        cols = pl.ds(c * part, part)
        return copy(
            y_send.at[p, :, cols],
            y_recv.at[src, :, cols],
            y_s.at[c, p],
            y_r.at[c, src],
            p,
            e,
        )

    for c in range(ex):
        y = jnp.dot(
            act, wd[:, c * part : (c + 1) * part], preferred_element_type=F32
        )
        y_send[:, :, c * part : (c + 1) * part] = (
            (y * weight).astype(BF16).reshape(dp, tokens, part)
        )
        exchange(dp, d, lambda p, c=c: y_copy(p, d, c))
    for c in range(ex):
        cols = slice(c * part, (c + 1) * part)
        got = y_send[d, :, cols].astype(F32)
        for o in range(1, dp):
            p = lax.rem(d + o, dp)
            y_copy(p, p, c).wait_recv()
            got += y_recv[p, :, cols].astype(F32)
        total[:, cols] = got
    total[:, pl.ds(pl.multiple_of(e * part, HD), part)] += hid[...]

    for k in range(ex):
        for c in range(pieces):
            fold[k, c * rows : (c + 1) * rows, :] = total[
                k * rows : (k + 1) * rows, c * piece : (c + 1) * piece
            ]
        z_send[k] = fold[k].astype(BF16)
    exchange(
        ex, e, lambda p: copy(z_send.at[p], z_recv.at[e], z_s.at[p], z_r.at[e], d, p)
    )
    result = fold[e]
    for o in range(1, ex):
        p = lax.rem(e + o, ex)
        copy(z_send.at[p], z_recv.at[p], z_s.at[p], z_r.at[p], d, p).wait_recv()
        result += z_recv[p].astype(F32)
    for c in range(pieces):
        out[:, c * piece : (c + 1) * piece] = result[c * rows : (c + 1) * rows].astype(
            out.dtype
        )

    for c in sends:
        c.wait_send()

    def a0_sent(o, c):
        a0_copy(o, False).wait_send()
        return c

    lax.fori_loop(1, n, a0_sent, 0)


def per_device(
    query,
    fresh_kv,
    cache,
    lengths,
    moves,
    residual,
    out_weight,
    norm_gain,
    w_gate,
    w_up,
    w_down,
    routes,
    gates,
):
    dp = lax.axis_size("dp")
    ex = lax.axis_size("expert")
    n = dp * ex
    rows, width = query.shape
    heads = width // HD
    hk = heads // ex
    part = width // ex
    tiles = part // HD
    tokens = rows * ex
    ff = w_gate.shape[-1]
    pieces = 16 // rows
    qrows = -(-(heads + 2 * KVH) // 16) * 16
    dma = pltpu.SemaphoreType.DMA
    vmem = pltpu.VMEM
    scratch = [
        vmem(cache.shape, BF16),
        vmem(out_weight.shape, BF16),
        vmem((width, ff), BF16),
        vmem((width, ff), BF16),
        vmem((ff, width), BF16),
        vmem((rows, qrows, HD), F32),
        vmem((qrows, HD), BF16),
        vmem((dp, qrows, HD), BF16),
        vmem((ex, rows, tiles + 1, HD), F32),
        vmem((tokens, tiles + 1, HD), F32),
        vmem((ex, rows - 1, hk, HD), F32),
        vmem((ex, hk, HD), F32),
        vmem((dp, ex, hk, HD), F32),
        vmem((tokens, hk, HD), F32),
        vmem((tokens, part), BF16),
        vmem((ex, tokens, part), BF16),
        vmem((ex, tokens, part), BF16),
        vmem((tokens, part), F32),
        vmem((tokens, part), BF16),
        vmem((tokens, HD), F32),
        vmem((dp * tokens, width), BF16),
        vmem((dp, ex, tokens, HD), F32),
        vmem((dp, tokens, width), BF16),
        vmem((dp, tokens, width), BF16),
        vmem((tokens, width), F32),
        vmem((ex, 16, width // pieces), F32),
        vmem((ex, 16, width // pieces), BF16),
        vmem((ex, 16, width // pieces), BF16),
        dma((5,)),
    ]
    for shape in (
        (dp,),
        (ex,),
        (ex,),
        (n,),
        (ex,),
        (ex,),
        (ex,),
        (dp,),
        (dp,),
        (ex, dp),
        (ex,),
    ):
        scratch += [dma(shape), dma(shape)]
    smem = pl.BlockSpec(memory_space=pltpu.SMEM)
    inside = pl.BlockSpec(memory_space=pltpu.VMEM)
    outside = pl.BlockSpec(memory_space=pl.ANY)
    return pl.pallas_call(
        functools.partial(layer_kernel, dp, ex),
        out_shape=jax.ShapeDtypeStruct(query.shape, BF16),
        in_specs=[smem] * 2 + [inside] * 6 + [outside] * 5,
        out_specs=inside,
        scratch_shapes=scratch,
        compiler_params=pltpu.CompilerParams(
            collective_id=0,
            has_side_effects=True,
            vmem_limit_bytes=56 * 1024 * 1024,
        ),
    )(
        lengths,
        moves,
        query,
        fresh_kv,
        residual,
        routes,
        gates,
        norm_gain.reshape(1, width),
        cache,
        out_weight,
        w_gate,
        w_up,
        w_down,
    )


def solution(mesh):
    placed = (
        P(("groups", "dp", "expert"), None),
        P(("groups", "dp", "expert"), None),
        P(("groups", "dp", "expert"), None, None),
        P(("groups", "dp", "expert")),
        P("groups", None),
        P(("groups", "dp", "expert"), None),
        P("expert", None),
        P(),
        P("dp", None, "expert"),
        P("dp", None, "expert"),
        P("dp", "expert", None),
        P(("groups", "dp", "expert"), None),
        P(("groups", "dp", "expert"), None),
    )
    return jax.shard_map(
        per_device,
        mesh=mesh,
        in_specs=placed,
        out_specs=P(("groups", "dp", "expert"), None),
        check_vma=False,
    )
```

time: 162 us -> 51.5 us (0.32)
  waiting for transfers between devices: 69.8 us -> 0 us
  Pallas kernels: 0 us -> 47.1 us
  blocking collectives: 20 us -> 0 us
  between operations: 16.2 us -> 0.01 us
  starting transfers between devices: 14.4 us -> 0 us
  local copies, waits for them, and re-layouts: 18.1 us -> 4.04 us
  matrix products: 13.5 us -> 0 us
  other arithmetic: 9.41 us -> 0 us
    pallas_call x0 -> x1, Pallas kernels: none -> 47.1 us  [per_device(): pl.pallas_call(functools.partial(layer_kernel, dp, ex), out_shape=jax.Sha...]
    all_to_all x3 -> x0, waiting for transfers between devices: 38.3 us -> none  [the longest x1 17.1 us: per_device(): lax.all_to_all(outgoing, 'dp', split_axis=0, concat_axis=0, tiled=True)]
    unnamed x2 -> x0, waiting for transfers between devices: 31.5 us -> none
    all_to_all x1 -> x0, blocking collectives: 20 us -> none  [per_device(): lax.all_to_all(spread, ('dp', 'expert'), split_axis=0, concat_axis=0, til...]
    all_to_all x3 -> x0, starting transfers between devices: 14.4 us -> none  [the longest x1 5.67 us: per_device(): lax.all_to_all(attended, 'expert', split_axis=1, concat_axis=0, tiled=True)]
    dot_general x8 -> x0, matrix products: 13.5 us -> none  [the longest x1 5.29 us: per_device(): jnp.dot(blocks, out_weight, preferred_element_type=jnp.float32)]
    reduce_sum x8 -> x0, other arithmetic: 4.23 us -> none  [the longest x1 1.35 us: per_device(): summed = jnp.sum(returned_rows.reshape(dp_count, ex_count, CAP, D), axis=1)]
    broadcast_in_dim x4 -> x0, local copies, waits for them, and re-layouts: 4.19 us -> none  [the longest x2 3.92 us: per_device(): jnp.where((peer_ids == target)[:, None, None], cache[0][None], jnp.zeros(...]
  transfers between devices with their start and end apart: 4 -> 0, of which waited for: 4 -> 0; matrix products, arithmetic and copies ran while one was open for 5% -> 0% of each run, Pallas kernels for 0% -> 0%
where the time goes in v1:
time: 51.5 us; the launch traced here: 51.2 us
  Pallas kernels  47.1 us (91%)
  local copies, waits for them, and re-layouts  4.04 us (8%)
    pallas_call x1, Pallas kernels, per_device(): pl.pallas_call(functools.partial(layer_kernel, dp, ex), out_shape=jax.Sha...  47.1 us
    unnamed x3, local copies, waits for them, and re-layouts  4.04 us

profile of v1, /device:TPU:0, one launch (start us, length us, event | category | flops | bytes accessed | tf_op | source)
XLA Modules:
  0.0 51.2 jit_solution(4365854001114788534)
XLA Ops:
  0.0 1.3 %copy.14.routes = s32[4,2]{1,0:T(4,128)} copy(s32[4,2]{0,1:T(2,128)} %param.24) | data formatting | bytes 64 | tf_op args[11]
  1.3 1.3 %copy.15.gates = f32[4,2]{1,0:T(4,128)} copy(f32[4,2]{0,1:T(2,128)} %param.25) | data formatting | bytes 64 | tf_op args[12]
  2.7 47.1 %shard_map.127 = bf16[4,4096]{1,0:T(4,128)(2,1)} custom-call(s32[4]{0:T(128)} %lengths.1, s32[4,4]{1,0:T(4,128)} %moves.1, bf16[4,4096]{1,0:T(4,128)(2,1)} %query.1, bf16[4,512]{1,0:T(4,128)(2,1)} %fresh.1, bf16[4,4096]{1,0:T(4,128)(2,1)} %residual.1, s32[4,2]{1,0:T(4,128)} %copy.14.routes, f32[4,2]{1,0:T(4,128)} %copy.15.gates, f32[1,4096]{1,0:T(1,128)} %bitcast.1, ...), custom_call_target="tpu_custom_call" | custom-call | tf_op jit(solution)/shard_map/pallas_call | solution.py:501
  49.8 1.4 %copy.17 = bf16[4,4096]{1,0:T(4,128)(2,1)} copy(bf16[4,4096]{1,0:T(4,128)(2,1)} %shard_map.127) | data formatting | bytes 65536

commit v2 on v1

--- a/solution.py
+++ b/solution.py
@@ -19,11 +19,11 @@
     ex,
     lengths,
     moves,
+    routes,
+    gates,
     query,
     fresh,
     residual,
-    routes,
-    gates,
     gain,
     cache_hbm,
     wo_hbm,
@@ -51,10 +51,15 @@
     hid,
     x_send,
     s_send,
+    s_part,
     x_all,
     s_all,
+    gate_sum,
+    up_sum,
     y_send,
     y_recv,
+    v_send,
+    v_recv,
     total,
     fold,
     z_send,
@@ -76,10 +81,13 @@
     s_r,
     x2_s,
     x2_r,
+    x3_s,
     s2_s,
     s2_r,
     y_s,
     y_r,
+    v_s,
+    v_r,
     z_s,
     z_r,
 ):
@@ -96,9 +104,9 @@
     part = width // ex
     tiles = part // HD
     tokens = rows * ex
-    top = routes.shape[1]
+    top = routes.shape[0]
     pieces = 16 // rows
-    piece = width // pieces
+    piece = part // pieces
 
     def copy(src, dst, ss, rs, dd, ee):
         return pltpu.make_async_remote_copy(
@@ -143,9 +151,12 @@
     q_send[...] = qf[0].astype(BF16)
 
     lane = lax.broadcasted_iota(jnp.int32, (rows, HD), 1)
+    line = lax.broadcasted_iota(jnp.int32, (rows, HD), 0)
     table = jnp.zeros((rows, HD), F32)
-    for k in range(top):
-        table += jnp.where(lane == routes[:, k : k + 1], gates[:, k : k + 1], 0.0)
+    for r in range(rows):
+        for k in range(top):
+            named = (line == r) & (lane == routes[k, r])
+            table += jnp.where(named, gates[k, r], 0.0)
     for k in range(ex):
         for j in range(tiles):
             r_send[k, :, j, :] = residual[
@@ -210,13 +221,10 @@
 
     local[0].wait()
 
-    def stay(r, c):
+    for r in range(1, rows):
         att = attend(r, qf[r])
         for k in range(ex):
             a_send[k, r - 1] = att[k * hk : (k + 1) * hk]
-        return c
-
-    lax.fori_loop(1, rows, stay, 0)
     exchange(
         ex,
         e,
@@ -315,101 +323,174 @@
         hidden * gain[:, pl.ds(pl.multiple_of(e * part, HD), part)]
     ).astype(BF16)
 
+    core = lax.rem(d, 2)
+    chip = d // 2
+    chips = dp // 2
+    twin = d + 1 - 2 * core
+
     def x_at(dd, ee):
         return x_all.at[
             pl.ds(pl.multiple_of(dd * tokens, 16), tokens),
             pl.ds(pl.multiple_of(ee * part, HD), part),
         ]
 
+    def x_twin(dd, ee, to):
+        return copy(
+            x_at(dd, ee), x_at(dd, ee), x2_s.at[dd, ee], x2_r.at[dd, ee], to, e
+        )
+
+    def x_chip(p, dd, ee):
+        to = p * 2 + core
+        return copy(
+            x_at(dd, ee), x_at(dd, ee), x3_s.at[p, ee], x2_r.at[dd, ee], to, e
+        )
+
+    def spread(ee):
+        made = [x_chip(lax.rem(chip + o, chips), d, ee) for o in range(1, chips)]
+        made.append(x_twin(d, ee, twin))
+        for c in made:
+            c.start()
+        sends.extend(made)
+
     exchange(ex, e, lambda p: copy(x_send, x_at(d, e), x_s.at[p], x_r.at[e], d, p))
-    exchange(
-        ex, e, lambda p: copy(s_send, s_all.at[d, e], s_s.at[p], s_r.at[e], d, p)
-    )
+    exchange(ex, e, lambda p: copy(s_send, s_part.at[e], s_s.at[p], s_r.at[e], d, p))
     x_at(d, e)[...] = x_send[...]
-    s_all[d, e] = s_send[...]
+    spread(e)
+    s_part[e] = s_send[...]
     for o in range(1, ex):
         p = lax.rem(e + o, ex)
         copy(x_send, x_at(d, p), x_s.at[p], x_r.at[p], d, p).wait_recv()
-        copy(s_send, s_all.at[d, p], s_s.at[p], s_r.at[p], d, p).wait_recv()
-
-    def x_rows(dd):
-        return x_all.at[pl.ds(pl.multiple_of(dd * tokens, 16), tokens)]
-
-    exchange(dp, d, lambda p: copy(x_rows(d), x_rows(d), x2_s.at[p], x2_r.at[d], p, e))
+        spread(p)
+    for o in range(1, ex):
+        p = lax.rem(e + o, ex)
+        copy(s_send, s_part.at[p], s_s.at[p], s_r.at[p], d, p).wait_recv()
+    square_sum = s_part[0]
+    for k in range(1, ex):
+        square_sum += s_part[k]
+    s_all[d] = jnp.where(
+        last, lax.rsqrt(square_sum / width + NORM_EPS), r_recv[:, tiles, :]
+    )
     exchange(
         dp, d, lambda p: copy(s_all.at[d], s_all.at[d], s2_s.at[p], s2_r.at[d], p, e)
     )
+
     local[2].wait()
     local[3].wait()
+    every = dp * tokens
+    for o in range(ex):
+        k = lax.rem(e + o, ex)
+        for q in range(1, chips):
+            p = lax.rem(chip + q, chips)
+            dd = p * 2 + core
+            x_chip(p, dd, k).wait_recv()
+            c = x_twin(dd, k, twin)
+            c.start()
+            sends.append(c)
+        for q in range(chips):
+            x_twin(lax.rem(chip + q, chips) * 2 + 1 - core, k, twin).wait_recv()
+        block = x_all[:, pl.ds(pl.multiple_of(k * part, HD), part)]
+        lines = pl.ds(pl.multiple_of(k * part, 16), part)
+        g = jnp.dot(block, wg[lines, :], preferred_element_type=F32)
+        u = jnp.dot(block, wu[lines, :], preferred_element_type=F32)
+        gate_sum[...] = g if o == 0 else gate_sum[...] + g
+        up_sum[...] = u if o == 0 else up_sum[...] + u
     for o in range(1, dp):
         p = lax.rem(d + o, dp)
-        copy(x_rows(p), x_rows(p), x2_s.at[p], x2_r.at[p], p, e).wait_recv()
         copy(s_all.at[p], s_all.at[p], s2_s.at[p], s2_r.at[p], p, e).wait_recv()
-
-    every = dp * tokens
     wide_lane = lax.broadcasted_iota(jnp.int32, (every, HD), 1)
-    stats = s_all[:, 0].reshape(every, HD)
+    stats = s_all[...].reshape(every, HD)
     weight = jnp.sum(jnp.where(wide_lane == d, stats, 0.0), axis=-1, keepdims=True)
-    for k in range(1, ex):
-        stats += s_all[:, k].reshape(every, HD)
-    mean = (
-        jnp.sum(jnp.where(wide_lane == HD - 1, stats, 0.0), axis=-1, keepdims=True)
-        / width
-    )
-    scale = lax.rsqrt(mean + NORM_EPS)
-    gate_val = jnp.dot(x_all[...], wg[...], preferred_element_type=F32) * scale
-    up_val = jnp.dot(x_all[...], wu[...], preferred_element_type=F32) * scale
-    act = (gate_val / (1.0 + jnp.exp(-gate_val)) * up_val).astype(BF16)
+    scale = stats[:, HD - 1 :]
+    gate_val = gate_sum[...] * scale
+    act = (gate_val / (1.0 + jnp.exp(-gate_val)) * (up_sum[...] * scale)).astype(BF16)
 
     local[4].wait()
 
-    def y_copy(p, src, c):
+    def y_twin(c):
         cols = pl.ds(c * part, part)
         return copy(
-            y_send.at[p, :, cols],
-            y_recv.at[src, :, cols],
-            y_s.at[c, p],
-            y_r.at[c, src],
-            p,
+            y_send.at[1 - core, :, :, cols],
+            y_recv.at[:, :, cols],
+            y_s.at[c],
+            y_r.at[c],
+            twin,
             e,
         )
 
-    for c in range(ex):
+    def v_copy(p, src, c):
+        cols = pl.ds(c * part, part)
+        return copy(
+            v_send.at[p, :, cols],
+            v_recv.at[src, :, cols],
+            v_s.at[c, p],
+            v_r.at[c, src],
+            p * 2 + core,
+            e,
+        )
+
+    def z_copy(p, src, c):
+        return copy(
+            z_send.at[c, p], z_recv.at[c, src], z_s.at[c, p], z_r.at[c, src], d, p
+        )
+
+    def down(c):
         y = jnp.dot(
             act, wd[:, c * part : (c + 1) * part], preferred_element_type=F32
-        )
-        y_send[:, :, c * part : (c + 1) * part] = (
-            (y * weight).astype(BF16).reshape(dp, tokens, part)
-        )
-        exchange(dp, d, lambda p, c=c: y_copy(p, d, c))
+        ) * weight
+        for dd in range(dp):
+            y_send[dd % 2, dd // 2, :, c * part : (c + 1) * part] = y[
+                dd * tokens : (dd + 1) * tokens
+            ].astype(BF16)
+        t = y_twin(c)
+        t.start()
+        sends.append(t)
+
+    def over_cores(c):
+        cols = slice(c * part, (c + 1) * part)
+        y_twin(c).wait_recv()
+        for o in range(1, chips):
+            p = lax.rem(chip + o, chips)
+            v_send[p, :, cols] = (
+                y_send[core, p, :, cols].astype(F32) + y_recv[p, :, cols].astype(F32)
+            ).astype(BF16)
+            t = v_copy(p, chip, c)
+            t.start()
+            sends.append(t)
+
+    def over_chips(c):
+        cols = slice(c * part, (c + 1) * part)
+        got = y_send[core, chip, :, cols].astype(F32) + y_recv[chip, :, cols].astype(F32)
+        got += jnp.where(e == c, hid[...], 0.0)
+        for o in range(1, chips):
+            p = lax.rem(chip + o, chips)
+            v_copy(p, p, c).wait_recv()
+            got += v_recv[p, :, cols].astype(F32)
+        total[...] = got
+        for k in range(ex):
+            for i in range(pieces):
+                fold[c, k, i * rows : (i + 1) * rows, :] = total[
+                    k * rows : (k + 1) * rows, i * piece : (i + 1) * piece
+                ]
+            z_send[c, k] = fold[c, k].astype(BF16)
+        exchange(ex, e, lambda p: z_copy(p, e, c))
+
     for c in range(ex):
-        cols = slice(c * part, (c + 1) * part)
-        got = y_send[d, :, cols].astype(F32)
-        for o in range(1, dp):
-            p = lax.rem(d + o, dp)
-            y_copy(p, p, c).wait_recv()
-            got += y_recv[p, :, cols].astype(F32)
-        total[:, cols] = got
-    total[:, pl.ds(pl.multiple_of(e * part, HD), part)] += hid[...]
-
-    for k in range(ex):
-        for c in range(pieces):
-            fold[k, c * rows : (c + 1) * rows, :] = total[
-                k * rows : (k + 1) * rows, c * piece : (c + 1) * piece
-            ]
-        z_send[k] = fold[k].astype(BF16)
-    exchange(
-        ex, e, lambda p: copy(z_send.at[p], z_recv.at[e], z_s.at[p], z_r.at[e], d, p)
-    )
-    result = fold[e]
-    for o in range(1, ex):
-        p = lax.rem(e + o, ex)
-        copy(z_send.at[p], z_recv.at[p], z_s.at[p], z_r.at[p], d, p).wait_recv()
-        result += z_recv[p].astype(F32)
-    for c in range(pieces):
-        out[:, c * piece : (c + 1) * piece] = result[c * rows : (c + 1) * rows].astype(
-            out.dtype
-        )
+        down(c)
+        if c:
+            over_cores(c - 1)
+    over_cores(ex - 1)
+    for c in range(ex):
+        over_chips(c)
+    for c in range(ex):
+        result = fold[c, e]
+        for o in range(1, ex):
+            p = lax.rem(e + o, ex)
+            z_copy(p, p, c).wait_recv()
+            result += z_recv[c, p].astype(F32)
+        for i in range(pieces):
+            out[:, c * part + i * piece : c * part + (i + 1) * piece] = result[
+                i * rows : (i + 1) * rows
+            ].astype(out.dtype)
 
     for c in sends:
         c.wait_send()
@@ -471,29 +552,25 @@
         vmem((tokens, part), F32),
         vmem((tokens, part), BF16),
         vmem((tokens, HD), F32),
+        vmem((ex, tokens, HD), F32),
         vmem((dp * tokens, width), BF16),
-        vmem((dp, ex, tokens, HD), F32),
-        vmem((dp, tokens, width), BF16),
-        vmem((dp, tokens, width), BF16),
-        vmem((tokens, width), F32),
-        vmem((ex, 16, width // pieces), F32),
-        vmem((ex, 16, width // pieces), BF16),
-        vmem((ex, 16, width // pieces), BF16),
+        vmem((dp, tokens, HD), F32),
+        vmem((dp * tokens, ff), F32),
+        vmem((dp * tokens, ff), F32),
+        vmem((2, dp // 2, tokens, width), BF16),
+        vmem((dp // 2, tokens, width), BF16),
+        vmem((dp // 2, tokens, width), BF16),
+        vmem((dp // 2, tokens, width), BF16),
+        vmem((tokens, part), F32),
+        vmem((ex, ex, 16, part // pieces), F32),
+        vmem((ex, ex, 16, part // pieces), BF16),
+        vmem((ex, ex, 16, part // pieces), BF16),
         dma((5,)),
     ]
-    for shape in (
-        (dp,),
-        (ex,),
-        (ex,),
-        (n,),
-        (ex,),
-        (ex,),
-        (ex,),
-        (dp,),
-        (dp,),
-        (ex, dp),
-        (ex,),
-    ):
+    for shape in ((dp,), (ex,), (ex,), (n,), (ex,), (ex,), (ex,), (dp, ex)):
+        scratch += [dma(shape), dma(shape)]
+    scratch.append(dma((dp // 2, ex)))
+    for shape in ((dp,), (ex,), (ex, dp // 2), (ex, ex)):
         scratch += [dma(shape), dma(shape)]
     smem = pl.BlockSpec(memory_space=pltpu.SMEM)
     inside = pl.BlockSpec(memory_space=pltpu.VMEM)
@@ -501,7 +578,7 @@
     return pl.pallas_call(
         functools.partial(layer_kernel, dp, ex),
         out_shape=jax.ShapeDtypeStruct(query.shape, BF16),
-        in_specs=[smem] * 2 + [inside] * 6 + [outside] * 5,
+        in_specs=[smem] * 4 + [inside] * 4 + [outside] * 5,
         out_specs=inside,
         scratch_shapes=scratch,
         compiler_params=pltpu.CompilerParams(
@@ -512,11 +589,11 @@
     )(
         lengths,
         moves,
+        routes.T,
+        gates.T,
         query,
         fresh_kv,
         residual,
-        routes,
-        gates,
         norm_gain.reshape(1, width),
         cache,
         out_weight,

time: 51.5 us -> 45.1 us (0.88)
  Pallas kernels: 47.1 us -> 43.4 us
  local copies, waits for them, and re-layouts: 4.04 us -> 1.39 us
    pallas_call x1, Pallas kernels: 47.1 us -> 43.4 us  [per_device(): pl.pallas_call(functools.partial(layer_kernel, dp, ex), out_shape=jax.Sha...]
    unnamed x3 -> x1, local copies, waits for them, and re-layouts: 4.04 us -> 1.39 us
where the time goes in v2:
time: 45.1 us; the launch traced here: 44.8 us
  Pallas kernels  43.4 us (96%)
  local copies, waits for them, and re-layouts  1.39 us (3%)
    pallas_call x1, Pallas kernels, per_device(): pl.pallas_call(functools.partial(layer_kernel, dp, ex), out_shape=jax.Sha...  43.4 us
    unnamed x1, local copies, waits for them, and re-layouts  1.39 us

profile of v2, /device:TPU:0, one launch (start us, length us, event | category | flops | bytes accessed | tf_op | source)
XLA Modules:
  0.0 44.8 jit_solution(6914047779615744784)
XLA Ops:
  0.0 43.4 %shard_map.127 = bf16[4,4096]{1,0:T(4,128)(2,1)} custom-call(s32[4]{0:T(128)} %lengths.1, s32[4,4]{1,0:T(4,128)} %moves.1, s32[2,4]{1,0:T(2,128)} %bitcast.4, f32[2,4]{1,0:T(2,128)} %bitcast.5, bf16[4,4096]{1,0:T(4,128)(2,1)} %query.1, bf16[4,512]{1,0:T(4,128)(2,1)} %fresh.1, bf16[4,4096]{1,0:T(4,128)(2,1)} %residual.1, f32[1,4096]{1,0:T(1,128)} %bitcast.3, ...), custom_call_target="tpu_custom_call" | custom-call | tf_op jit(solution)/shard_map/pallas_call | solution.py:578
  43.4 1.4 %copy.15 = bf16[4,4096]{1,0:T(4,128)(2,1)} copy(bf16[4,4096]{1,0:T(4,128)(2,1)} %shard_map.127) | data formatting | bytes 65536
